TPU v7x, 32 devices: a whole 2x2x4 slice. The times are simulated.
32 devices in a mesh: grp: 2 (over x), band: 16 (over z, y, core).
Axes of the slice: x: 2, y: 2, z: 4, core: 2. Of those that a mesh axis runs over, the one named last changes fastest.
Arguments:
- opacity_deriv: bfloat16 [4, 1024, 4096], P('grp', None, 'band'), parts along dimension 0, may hold values from -6 to 6
- emission_deriv: bfloat16 [4, 1024, 4096], P('grp', None, 'band'), parts along dimension 0, may hold values from -0.09375 to 0.09375
- kernel_tiles: float32 [8, 128, 128], replicated, may hold values from 0.1 to 1
- tile_map: int32 [4, 8, 8], P('grp'), parts along dimension 0, may hold values from 0 to 7
- active_counts: int32 [4], P('grp'), parts along dimension 0, may hold values from 512 to 1024, as said below
Outputs:
- jacobian: float32 [1024, 4, 1024], P('band', 'grp'), parts along dimension 1
There are 2 independent parts, one for each index of `grp`. A program takes and returns all parts, laid end to end along the dimension named above; an argument that names none is the same for every part. Nothing has to cross between parts.
Inputs may be any that keep to these rules, and one draw needn't show every extreme that they name: `active_counts`: at least one line of each batch has all 1024 cells active.
All inputs are finite; a program needn't handle non-finite values.
Results may differ from a plain program's by a relative error of at most 0.0003.
Values may be sent and summed in bfloat16 or wider, within the bound.
A program may use at most 64 MiB of HBM per device.

v0:
```python
import jax
import jax.numpy as jnp
from jax import lax
from jax.sharding import PartitionSpec as P


def body(opacity_deriv, emission_deriv, kernel_tiles, tile_map, active_counts):
    cells = opacity_deriv.shape[1]
    kinds = kernel_tiles.shape[0]
    tile = kernel_tiles.shape[1]
    shards = lax.axis_size("band")
    row_count = cells // shards
    first_row = lax.axis_index("band") * row_count
    coupling = lax.psum_scatter(
        jnp.einsum(
            "lib,ljb->ilj", opacity_deriv, emission_deriv, preferred_element_type=jnp.float32
        ),
        "band",
        scatter_dimension=0,
        tiled=True,
    )
    my_rows = first_row + jnp.arange(row_count, dtype=jnp.int32)
    chosen = jnp.take(tile_map, my_rows // tile, axis=1)
    onehot = (chosen[..., None] == jnp.arange(kinds, dtype=jnp.int32)).astype(jnp.float32)
    tile_rows = jnp.take(kernel_tiles, my_rows % tile, axis=1)
    weight = jnp.einsum("lrqk,krt->rlqt", onehot, tile_rows, precision=lax.Precision.HIGHEST)
    weight = weight.reshape(row_count, onehot.shape[0], cells)
    columns = jnp.arange(cells, dtype=jnp.int32)
    same = (my_rows[:, None, None] == columns[None, None, :]).astype(jnp.float32)
    diagonal = jnp.sum(coupling * same, axis=2, keepdims=True)
    live = active_counts[None, :, None]
    inside = (my_rows[:, None, None] < live) & (columns[None, None, :] < live)
    result = weight * coupling - 2.0 * same * diagonal
    return jnp.where(inside, result, jnp.zeros_like(result))


def solution(mesh):
    return jax.shard_map(
        body,
        mesh=mesh,
        in_specs=(
            P("grp", None, "band"),
            P("grp", None, "band"),
            P(),
            P("grp", None, None),
            P("grp"),
        ),
        out_specs=P("band", "grp", None),
        check_vma=False,
    )
```

profile of v0, /device:TPU:0, one launch (start us, length us, event | category | flops | bytes accessed | tf_op | source)
XLA Modules:
  0.0 209.6 jit_solution(5923213821196019512)
XLA Ops:
  6.5 0.0 copy-start
  6.5 0.0 all-reduce.3.cloned.1.call-start
  6.5 1.2 copy-done
  7.8 5.7 %convolution_bitcast_fusion = f32[1024,2,1024]{0,2,1:T(8,128)} fusion(bf16[2,1024,256]{2,1,0:T(8,128)(2,1)S(1)} %copy-done, bf16[2,1024,256]{2,1,0:T(8,128)(2,1)} %param.5), kind=kOutput, calls=%fused_computation.3 | convolution fusion | flops 1073741824 | bytes 10485760 | tf_op jit(solution)/shard_map/lib,ljb->ilj/dot_general | solution.py:15
  13.5 13.4 %copy.16 = f32[1024,2,1024]{2,1,0:T(2,128)} copy(f32[1024,2,1024]{0,2,1:T(8,128)} %convolution_bitcast_fusion) | data formatting | bytes 16777216 | tf_op jit(solution)/shard_map/lib,ljb->ilj/transpose | solution.py:15
  26.9 0.0 copy-start.1
  26.9 0.0 copy-start.2
  26.9 0.0 copy-start.4
  26.9 0.0 copy-start.3
  26.9 0.0 all-reduce.3.cloned.1.call-update
  26.9 0.6 copy-done.1
  27.6 0.6 gather_fusion
  28.2 0.1 select_bitcast_fusion.1
  28.3 0.1 copy.14
  28.4 0.0 copy-done.2
  28.4 1.0 gather_fusion.1
  29.4 0.1 select_bitcast_fusion
  29.5 0.5 fusion.4
  30.0 0.3 reshape.203
  30.3 0.0 copy-done.4
  30.3 0.6 dynamic-slice
  31.6 0.0 copy-done.3
  31.6 0.1 iota_compare_fusion.3
  31.6 0.1 broadcast_compare_fusion
  31.7 0.1 fusion.9
  31.8 0.1 fusion.10
  31.9 167.7 %all-reduce.3.cloned.1.call-done = f32[1024,2,1024]{2,1,0:T(2,128)} async-done(((f32[1024,2,1024]{2,1,0:T(2,128)}), f32[1024,2,1024]{2,1,0:T(2,128)}) %all-reduce.3.cloned.1.call-update) | async-done | bytes 8388624
  199.6 3.1 %fusion.3 = f32[64,2,1024]{2,1,0:T(2,128)} fusion(f32[64,2,1024]{2,1,0:T(2,128)S(1)} %reshape.203, pred[2,1024]{1,0:T(4,128)(4,1)S(1)} %iota_compare_fusion.3, pred[64,2]{1,0:T(8,128)(4,1)S(1)} %broadcast_compare_fusion, f32[1024,2,1024]{2,1,0:T(2,128)} %all-reduce.3.cloned.1.call-done, u32[]{:T(128)S(6)} %multiply.1, f32[64,1024]{1,0:T(8,128)S(1)} %fusion.9, ...), kind=kOutput, calls=%fused_computation.6 | output fusion | flops 787583 | bytes 2624640 | tf_op jit(solution)/shard_map/mul | solution.py:33
  (5 shorter events, 0.0 us)
Async XLA Ops:
  6.5 1.2 copy-start
  6.5 193.1 %all-reduce.3.cloned.1.call-start = ((), (), s32[]{:S(2)}) async-start(), calls=%async_computation | async-start | bytes 16777216
  26.9 0.7 copy-start.1
  26.9 1.5 copy-start.2
  26.9 3.4 %copy-start.4 = (u32[32]{0:T(128)S(1)}, u32[32]{0:T(128)}, u32[]{:S(2)}) copy-start(u32[32]{0:T(128)} %constant.71) | copy-start | bytes 388
  26.9 4.7 %copy-start.3 = (s32[2]{0:T(128)S(1)}, s32[2]{0:T(128)}, u32[]{:S(2)}) copy-start(s32[2]{0:T(128)} %param.9) | copy-start | bytes 28
Sparse Core Ops, SparseCore 0:
  27.0 172.5 all-reduce.2
where the time goes:
time: 210 us
  waiting for transfers between devices  168 us (80%)
  local copies, waits for them, and re-layouts  17.8 us (8%)
  between operations  14.2 us (7%)
  matrix products  6.26 us (3%)
  other arithmetic  3.61 us (2%)
    unnamed x2, waiting for transfers between devices  168 us
    transpose x1, local copies, waits for them, and re-layouts, body(): jnp.einsum('lib,ljb->ilj', opacity_deriv, emission_deriv, preferred_eleme...  13.4 us
    dot_general x1, matrix products, body(): jnp.einsum('lib,ljb->ilj', opacity_deriv, emission_deriv, preferred_eleme...  5.73 us
  transfers between devices with their start and end apart: 1, of which 1 were waited for; matrix products, arithmetic and copies ran while one was open for 2% of the time, Pallas kernels for 0%

commit v1 on v0

--- a/solution.py
+++ b/solution.py
@@ -1,10 +1,19 @@
+import functools
+
 import jax
 import jax.numpy as jnp
 from jax import lax
+from jax.experimental import pallas as pl
+from jax.experimental.pallas import tpu as pltpu
 from jax.sharding import PartitionSpec as P
 
-
-def body(opacity_deriv, emission_deriv, kernel_tiles, tile_map, active_counts):
+MESH = pl.DeviceIdType.MESH
+TOP = 32767.0
+TINY = 1e-30
+WIDTH = 256
+
+
+def plain_body(opacity_deriv, emission_deriv, kernel_tiles, tile_map, active_counts):
     cells = opacity_deriv.shape[1]
     kinds = kernel_tiles.shape[0]
     tile = kernel_tiles.shape[1]
@@ -34,7 +43,241 @@
     return jnp.where(inside, result, jnp.zeros_like(result))
 
 
+def encode(block):
+    top = jnp.maximum(jnp.max(jnp.abs(block), axis=0, keepdims=True), TINY)
+    coded = jnp.round(block * (TOP / top)).astype(jnp.int32).astype(jnp.int16)
+    return coded, top * (1.0 / TOP)
+
+
+def decode(coded, scale):
+    return coded.astype(jnp.int32).astype(jnp.float32) * scale
+
+
+def product(left, right):
+    return lax.dot_general(
+        left, right, (((1,), (1,)), ((), ())), preferred_element_type=jnp.float32
+    )
+
+
+def kernel(
+    op_ref, em_ref, kt_ref, tm_ref, ac_ref, out_ref,
+    a_own, a_mate, b_own, b_mate, tiles,
+    y_out, y_out_scale, y_in, y_in_scale,
+    z_out, z_out_scale, z_in, z_in_scale, total,
+    own_sem, mate_send, mate_recv, y_send, y_recv, z_send, z_recv,
+):
+    lines, cells = em_ref.shape[0], em_ref.shape[1]
+    rows = op_ref.shape[3]
+    tile = kt_ref.shape[2]
+    depth = total.shape[0] // lines
+    levels = op_ref.shape[1] // 2
+    me = lax.axis_index("band")
+    core = lax.rem(me, 2)
+    y = lax.rem(me // 2, 2)
+    z = me // 4
+    mate = z * 4 + y * 2 + (1 - core)
+    across = z * 4 + (1 - y) * 2 + core
+    z_of = [lax.rem(z + d, levels) for d in range(levels)]
+    along = [z_of[d] * 4 + y * 2 + core for d in range(levels)]
+
+    own_copies = []
+    for l in range(lines):
+        own_copies.append(
+            (
+                pltpu.make_async_copy(op_ref.at[l, :, core], a_own.at[l], own_sem.at[l, 0]),
+                pltpu.make_async_copy(em_ref.at[l], b_own.at[l], own_sem.at[l, 1]),
+            )
+        )
+    tile_copy = pltpu.make_async_copy(
+        kt_ref.at[:, pl.ds(pl.multiple_of(core * rows, rows), rows), :], tiles, own_sem.at[0, 2]
+    )
+    for pair in own_copies:
+        for copy in pair:
+            copy.start()
+    tile_copy.start()
+
+    barrier = pltpu.get_barrier_semaphore()
+    peers = [mate, across] + along[1:]
+    for peer in peers:
+        pl.semaphore_signal(barrier, inc=1, device_id={"band": peer}, device_id_type=MESH)
+    pl.semaphore_wait(barrier, len(peers))
+
+    mate_copies = []
+    for l in range(lines):
+        mate_copies.append(
+            (
+                pltpu.make_async_remote_copy(
+                    op_ref.at[l, :, 1 - core], a_mate.at[l], mate_send.at[l, 0], mate_recv.at[l, 0],
+                    device_id={"band": mate}, device_id_type=MESH,
+                ),
+                pltpu.make_async_remote_copy(
+                    em_ref.at[l], b_mate.at[l], mate_send.at[l, 1], mate_recv.at[l, 1],
+                    device_id={"band": mate}, device_id_type=MESH,
+                ),
+            )
+        )
+    for pair in mate_copies:
+        for copy in pair:
+            copy.start()
+
+    def partial_sum(l, column, side):
+        left_own = jnp.concatenate([a_own[l, z_of[d] * 2 + side] for d in range(levels)], axis=0)
+        left_mate = jnp.concatenate([a_mate[l, z_of[d] * 2 + side] for d in range(levels)], axis=0)
+        span = pl.ds(column, WIDTH)
+        return product(left_own, b_own[l, span, :]) + product(left_mate, b_mate[l, span, :])
+
+    def y_copies(step):
+        return (
+            pltpu.make_async_remote_copy(
+                y_out.at[step], y_in.at[step], y_send.at[step, 0], y_recv.at[step, 0],
+                device_id={"band": across}, device_id_type=MESH,
+            ),
+            pltpu.make_async_remote_copy(
+                y_out_scale.at[step], y_in_scale.at[step], y_send.at[step, 1], y_recv.at[step, 1],
+                device_id={"band": across}, device_id_type=MESH,
+            ),
+        )
+
+    def z_copies(step, d):
+        return (
+            pltpu.make_async_remote_copy(
+                z_out.at[step, d - 1], z_in.at[step, d - 1],
+                z_send.at[step, d - 1, 0], z_recv.at[step, d - 1, 0],
+                device_id={"band": along[d]}, device_id_type=MESH,
+            ),
+            pltpu.make_async_remote_copy(
+                z_out_scale.at[step, d - 1], z_in_scale.at[step, d - 1],
+                z_send.at[step, d - 1, 1], z_recv.at[step, d - 1, 1],
+                device_id={"band": along[d]}, device_id_type=MESH,
+            ),
+        )
+
+    for l in range(lines):
+        for copy in own_copies[l] + mate_copies[l]:
+            copy.wait()
+
+        @pl.loop(0, depth)
+        def _(part):
+            step = l * depth + part
+            column = pl.multiple_of(part * WIDTH, WIDTH)
+            sums = partial_sum(l, column, 1 - y)
+            for d in range(levels):
+                coded, scale = encode(sums[d * rows : (d + 1) * rows])
+                y_out[step, d] = coded
+                y_out_scale[step, d : d + 1] = scale
+            for copy in y_copies(step):
+                copy.start()
+
+    for l in range(lines):
+
+        @pl.loop(0, depth)
+        def _(part):
+            step = l * depth + part
+            column = pl.multiple_of(part * WIDTH, WIDTH)
+            sums = partial_sum(l, column, y)
+            for copy in y_copies(step):
+                copy.wait()
+            for d in list(range(1, levels)) + [0]:
+                block = sums[d * rows : (d + 1) * rows] + decode(
+                    y_in[step, d], y_in_scale[step, d : d + 1]
+                )
+                if d == 0:
+                    total[step] = block
+                else:
+                    coded, scale = encode(block)
+                    z_out[step, d - 1] = coded
+                    z_out_scale[step, d - 1] = scale
+                    for copy in z_copies(step, d):
+                        copy.start()
+
+    tile_copy.wait()
+    row = lax.broadcasted_iota(jnp.int32, (rows, tile), 0) + me * rows
+    lane = lax.broadcasted_iota(jnp.int32, (rows, tile), 1)
+    for l in range(lines):
+        live = ac_ref[l]
+
+        @pl.loop(0, depth)
+        def _(part):
+            step = l * depth + part
+            block = total[step]
+            for d in range(1, levels):
+                for copy in z_copies(step, d):
+                    copy.wait()
+                block = block + decode(z_in[step, d - 1], z_in_scale[step, d - 1])
+            for s in range(WIDTH // tile):
+                coupling = block[:, s * tile : (s + 1) * tile]
+                at = part * (WIDTH // tile) + s
+                weight = tiles[tm_ref[l, me // 2, at]]
+                column = lane + at * tile
+                result = weight * coupling
+                result = jnp.where(row == column, result - 2.0 * coupling, result)
+                inside = (row < live) & (column < live)
+                start = pl.multiple_of(l * cells + at * tile, tile)
+                out_ref[:, pl.ds(start, tile)] = jnp.where(inside, result, 0.0)
+
+
+def fused_body(opacity_deriv, emission_deriv, kernel_tiles, tile_map, active_counts):
+    lines, cells, bands = opacity_deriv.shape
+    kinds, tile, _ = kernel_tiles.shape
+    shards = lax.axis_size("band")
+    rows = cells // shards
+    levels = shards // 4
+    groups = shards // 2
+    steps = lines * (cells // WIDTH)
+    vmem = pltpu.VMEM
+    dma = pltpu.SemaphoreType.DMA
+    half = jnp.bfloat16
+    wide = jnp.float32
+    out = pl.pallas_call(
+        kernel,
+        out_shape=jax.ShapeDtypeStruct((rows, lines * cells), wide),
+        in_specs=[pl.BlockSpec(memory_space=pl.ANY)] * 3
+        + [pl.BlockSpec(memory_space=pltpu.SMEM)] * 2,
+        out_specs=pl.BlockSpec(memory_space=pltpu.VMEM),
+        scratch_shapes=[
+            vmem((lines, groups, rows, bands), half),
+            vmem((lines, groups, rows, bands), half),
+            vmem((lines, cells, bands), half),
+            vmem((lines, cells, bands), half),
+            vmem((kinds, rows, tile), wide),
+            vmem((steps, levels, rows, WIDTH), jnp.int16),
+            vmem((steps, levels, WIDTH), wide),
+            vmem((steps, levels, rows, WIDTH), jnp.int16),
+            vmem((steps, levels, WIDTH), wide),
+            vmem((steps, levels - 1, rows, WIDTH), jnp.int16),
+            vmem((steps, levels - 1, 1, WIDTH), wide),
+            vmem((steps, levels - 1, rows, WIDTH), jnp.int16),
+            vmem((steps, levels - 1, 1, WIDTH), wide),
+            vmem((steps, rows, WIDTH), wide),
+            dma((lines, 3)),
+            dma((lines, 2)),
+            dma((lines, 2)),
+            dma((steps, 2)),
+            dma((steps, 2)),
+            dma((steps, levels - 1, 2)),
+            dma((steps, levels - 1, 2)),
+        ],
+        compiler_params=pltpu.CompilerParams(
+            collective_id=0, has_side_effects=True, vmem_limit_bytes=40 * 1024 * 1024
+        ),
+        cost_estimate=pl.CostEstimate(
+            flops=2 * lines * cells * cells * bands,
+            bytes_accessed=4 * lines * cells * bands,
+            transcendentals=0,
+        ),
+        name="band_sum",
+    )(
+        opacity_deriv.reshape(lines, groups, 2, rows, bands),
+        emission_deriv,
+        kernel_tiles,
+        tile_map,
+        active_counts,
+    )
+    return out.reshape(rows, lines, cells)
+
+
 def solution(mesh):
+    body = fused_body if mesh.shape["band"] == 16 else plain_body
     return jax.shard_map(
         body,
         mesh=mesh,

time: 210 us -> 45.3 us (0.22)
  waiting for transfers between devices: 168 us -> 0 us
  Pallas kernels: 0 us -> 38.9 us
  between operations: 14.2 us -> 0.01 us
  local copies, waits for them, and re-layouts: 17.8 us -> 6.07 us
  matrix products: 6.26 us -> 0 us
  other arithmetic: 3.61 us -> 0 us
    unnamed x2 -> x0, waiting for transfers between devices: 168 us -> none
    pallas_call x0 -> x1, Pallas kernels: none -> 38.9 us  [fused_body(): pl.pallas_call(kernel, out_shape=jax.ShapeDtypeStruct((rows, lines * cell...]
    transpose x1 -> x0, local copies, waits for them, and re-layouts: 13.4 us -> none  [body(): jnp.einsum('lib,ljb->ilj', opacity_deriv, emission_deriv, preferred_eleme...]
    dot_general x2 -> x0, matrix products: 6.26 us -> none  [the longest x1 5.73 us: body(): jnp.einsum('lib,ljb->ilj', opacity_deriv, emission_deriv, preferred_eleme...]
    mul x2 -> x0, other arithmetic: 3.16 us -> none  [body(): result = weight * coupling - 2.0 * same * diagonal]
    unnamed x11 -> x10, local copies, waits for them, and re-layouts: 2.44 us -> 4.84 us
  transfers between devices with their start and end apart: 1 -> 0, of which waited for: 1 -> 0; matrix products, arithmetic and copies ran while one was open for 2% -> 0% of each run, Pallas kernels for 0% -> 0%
where the time goes in v1:
time: 45.3 us; the launch traced here: 45 us
  Pallas kernels  38.9 us (86%)
  local copies, waits for them, and re-layouts  6.07 us (13%)
    pallas_call x1, Pallas kernels, fused_body(): pl.pallas_call(kernel, out_shape=jax.ShapeDtypeStruct((rows, lines * cell...  38.9 us
    unnamed x10, local copies, waits for them, and re-layouts  4.84 us
    reshape x1, local copies, waits for them, and re-layouts, fused_body(): return out.reshape(rows, lines, cells)  1.23 us

profile of v1, /device:TPU:0, one launch (start us, length us, event | category | flops | bytes accessed | tf_op | source)
XLA Modules:
  0.0 45.0 jit_solution(15010328849290054025)
XLA Ops:
  0.0 0.0 copy-start.4
  0.0 0.7 %copy-done.4 = s32[2]{0:T(128)S(1)} copy-done((s32[2]{0:T(128)S(1)}, s32[2]{0:T(128)}, u32[]{:S(2)}) %copy-start.4) | copy-done | bytes 32
  0.7 0.0 copy-start
  0.7 1.2 %copy-done = bf16[2,1024,256]{2,1,0:T(8,128)(2,1)S(1)} copy-done((bf16[2,1024,256]{2,1,0:T(8,128)(2,1)S(1)}, bf16[2,1024,256]{2,1,0:T(8,128)(2,1)}, u32[]{:S(2)}) %copy-start) | copy-done | bytes 1048600
  1.9 0.0 copy-start.1
  1.9 1.2 %copy-done.1 = bf16[2,1024,256]{2,1,0:T(8,128)(2,1)S(1)} copy-done((bf16[2,1024,256]{2,1,0:T(8,128)(2,1)S(1)}, bf16[2,1024,256]{2,1,0:T(8,128)(2,1)}, u32[]{:S(2)}) %copy-start.1) | copy-done | bytes 1048600
  3.1 0.0 copy-start.2
  3.1 1.0 %copy-done.2 = f32[8,128,128]{2,1,0:T(8,128)S(1)} copy-done((f32[8,128,128]{2,1,0:T(8,128)S(1)}, f32[8,128,128]{2,1,0:T(8,128)}, u32[]{:S(2)}) %copy-start.2) | copy-done | bytes 524312
  4.1 0.0 copy-start.3
  4.2 0.7 %copy-done.3 = s32[2,8,8]{2,1,0:T(8,128)S(1)} copy-done((s32[2,8,8]{2,1,0:T(8,128)S(1)}, s32[2,8,8]{2,1,0:T(8,128)}, u32[]{:S(2)}) %copy-start.3) | copy-done | bytes 536
  4.8 38.9 %band_sum.1 = f32[64,2048]{1,0:T(8,128)S(1)} custom-call(bf16[2,8,2,64,256]{4,3,2,1,0:T(8,128)(2,1)S(1)} %bitcast.1, bf16[2,1024,256]{2,1,0:T(8,128)(2,1)S(1)} %copy-done.1, f32[8,128,128]{2,1,0:T(8,128)S(1)} %copy-done.2, s32[2,8,8]{2,1,0:T(8,128)S(1)} %copy-done.3, s32[2]{0:T(128)S(1)} %copy-done.4), custom_call_target="tpu_custom_call" | custom-call | flops 1073741824 | bytes 2097152 | tf_op jit(solution)/shard_map/band_sum/pallas_call | solution.py:231
  43.8 1.2 %reshape.7 = f32[64,2,1024]{2,1,0:T(2,128)} reshape(f32[64,2048]{1,0:T(8,128)S(1)} %band_sum.1) | data formatting | bytes 1048576 | tf_op jit(solution)/shard_map/reshape | solution.py:276
Async XLA Ops:
  0.0 0.7 %copy-start.4 = (s32[2]{0:T(128)S(1)}, s32[2]{0:T(128)}, u32[]{:S(2)}) copy-start(s32[2]{0:T(128)} %ac_ref.1) | copy-start | bytes 28
  0.7 1.2 %copy-start = (bf16[2,1024,256]{2,1,0:T(8,128)(2,1)S(1)}, bf16[2,1024,256]{2,1,0:T(8,128)(2,1)}, u32[]{:S(2)}) copy-start(bf16[2,1024,256]{2,1,0:T(8,128)(2,1)} %param.5) | copy-start | bytes 3145732
  1.9 1.2 %copy-start.1 = (bf16[2,1024,256]{2,1,0:T(8,128)(2,1)S(1)}, bf16[2,1024,256]{2,1,0:T(8,128)(2,1)}, u32[]{:S(2)}) copy-start(bf16[2,1024,256]{2,1,0:T(8,128)(2,1)} %em_ref.1) | copy-start | bytes 3145732
  3.1 1.0 %copy-start.2 = (f32[8,128,128]{2,1,0:T(8,128)S(1)}, f32[8,128,128]{2,1,0:T(8,128)}, u32[]{:S(2)}) copy-start(f32[8,128,128]{2,1,0:T(8,128)} %kt_ref.1) | copy-start | bytes 1572868
  4.1 0.7 %copy-start.3 = (s32[2,8,8]{2,1,0:T(8,128)S(1)}, s32[2,8,8]{2,1,0:T(8,128)}, u32[]{:S(2)}) copy-start(s32[2,8,8]{2,1,0:T(8,128)} %tm_ref.1) | copy-start | bytes 1540

commit v2 on v1

v2 whole, which is shorter than its diff:
```python
import functools

import jax
import jax.numpy as jnp
from jax import lax
from jax.experimental import pallas as pl
from jax.experimental.pallas import tpu as pltpu
from jax.sharding import PartitionSpec as P

MESH = pl.DeviceIdType.MESH
TOP = 32767.0
TINY = 1e-30
WIDTH = 256
LAG_ALONG = 2
LAG_FINISH = 2
FAR_FIRST = (2, 1, 3, 0)


def plain_body(opacity_deriv, emission_deriv, kernel_tiles, tile_map, active_counts):
    cells = opacity_deriv.shape[1]
    kinds = kernel_tiles.shape[0]
    tile = kernel_tiles.shape[1]
    shards = lax.axis_size("band")
    row_count = cells // shards
    first_row = lax.axis_index("band") * row_count
    coupling = lax.psum_scatter(
        jnp.einsum(
            "lib,ljb->ilj", opacity_deriv, emission_deriv, preferred_element_type=jnp.float32
        ),
        "band",
        scatter_dimension=0,
        tiled=True,
    )
    my_rows = first_row + jnp.arange(row_count, dtype=jnp.int32)
    chosen = jnp.take(tile_map, my_rows // tile, axis=1)
    onehot = (chosen[..., None] == jnp.arange(kinds, dtype=jnp.int32)).astype(jnp.float32)
    tile_rows = jnp.take(kernel_tiles, my_rows % tile, axis=1)
    weight = jnp.einsum("lrqk,krt->rlqt", onehot, tile_rows, precision=lax.Precision.HIGHEST)
    weight = weight.reshape(row_count, onehot.shape[0], cells)
    columns = jnp.arange(cells, dtype=jnp.int32)
    same = (my_rows[:, None, None] == columns[None, None, :]).astype(jnp.float32)
    diagonal = jnp.sum(coupling * same, axis=2, keepdims=True)
    live = active_counts[None, :, None]
    inside = (my_rows[:, None, None] < live) & (columns[None, None, :] < live)
    result = weight * coupling - 2.0 * same * diagonal
    return jnp.where(inside, result, jnp.zeros_like(result))


def encode(block):
    top = jnp.maximum(jnp.max(jnp.abs(block), axis=0, keepdims=True), TINY)
    coded = jnp.round(block * (TOP / top)).astype(jnp.int32).astype(jnp.int16)
    return coded, top * (1.0 / TOP)


def decode(coded, scale):
    return coded.astype(jnp.int32).astype(jnp.float32) * scale


def product(left, right):
    return lax.dot_general(
        left, right, (((1,), (1,)), ((), ())), preferred_element_type=jnp.float32
    )


def kernel(
    op_ref, em_ref, kt_ref, map_ref, counts_ref, out_ref,
    a_own, a_mate, b_own, b_mate, tiles, tm_ref, ac_ref,
    y_out, y_out_scale, y_in, y_in_scale,
    z_out, z_out_scale, z_in, z_in_scale, total,
    own_sem, table_sem, a_send, a_recv, b_send, b_recv, y_send, y_recv, z_send, z_recv,
):
    lines, cells = em_ref.shape[0], em_ref.shape[1]
    levels, rows = op_ref.shape[1], op_ref.shape[4]
    tile = kt_ref.shape[2]
    steps = total.shape[0]
    depth = steps // lines
    me = lax.axis_index("band")
    core = lax.rem(me, 2)
    y = lax.rem(me // 2, 2)
    z = me // 4
    mate = z * 4 + y * 2 + (1 - core)
    across = z * 4 + (1 - y) * 2 + core
    z_of = [lax.rem(z + d, levels) for d in range(levels)]
    along = [z_of[d] * 4 + y * 2 + core for d in range(levels)]

    def place(step):
        l = step // depth
        return l, pl.multiple_of((step - l * depth) * WIDTH, WIDTH)

    own_copies = [
        pltpu.make_async_copy(op_ref.at[l, :, side, core], a_own.at[l, side], own_sem.at[l, side])
        for l in range(lines)
        for side in range(2)
    ] + [pltpu.make_async_copy(em_ref.at[l], b_own.at[l], own_sem.at[l, 2]) for l in range(lines)]
    table_copies = [
        pltpu.make_async_copy(
            kt_ref.at[:, pl.ds(pl.multiple_of(core * rows, rows), rows), :], tiles, table_sem.at[0]
        ),
        pltpu.make_async_copy(map_ref, tm_ref, table_sem.at[1]),
        pltpu.make_async_copy(counts_ref, ac_ref, table_sem.at[2]),
    ]

    barrier = pltpu.get_barrier_semaphore()
    peers = [mate, across] + along[1:]
    for peer in peers:
        pl.semaphore_signal(barrier, inc=1, device_id={"band": peer}, device_id_type=MESH)
    for copy in own_copies + table_copies:
        copy.start()
    pl.semaphore_wait(barrier, len(peers))

    def a_copy(l, side):
        return pltpu.make_async_remote_copy(
            op_ref.at[l, :, side, 1 - core], a_mate.at[l, side],
            a_send.at[l, side], a_recv.at[l, side],
            device_id={"band": mate}, device_id_type=MESH,
        )

    def b_copy(step):
        l, column = place(step)
        span = pl.ds(column, WIDTH)
        return pltpu.make_async_remote_copy(
            em_ref.at[l, span, :], b_mate.at[l, span, :], b_send.at[step], b_recv.at[step],
            device_id={"band": mate}, device_id_type=MESH,
        )

    def y_copies(step):
        return (
            pltpu.make_async_remote_copy(
                y_out.at[step], y_in.at[step], y_send.at[step, 0], y_recv.at[step, 0],
                device_id={"band": across}, device_id_type=MESH,
            ),
            pltpu.make_async_remote_copy(
                y_out_scale.at[step], y_in_scale.at[step], y_send.at[step, 1], y_recv.at[step, 1],
                device_id={"band": across}, device_id_type=MESH,
            ),
        )

    def z_copies(step, d):
        return (
            pltpu.make_async_remote_copy(
                z_out.at[step, d - 1], z_in.at[step, d - 1],
                z_send.at[step, d - 1, 0], z_recv.at[step, d - 1, 0],
                device_id={"band": along[d]}, device_id_type=MESH,
            ),
            pltpu.make_async_remote_copy(
                z_out_scale.at[step, d - 1], z_in_scale.at[step, d - 1],
                z_send.at[step, d - 1, 1], z_recv.at[step, d - 1, 1],
                device_id={"band": along[d]}, device_id_type=MESH,
            ),
        )

    for l in range(lines):
        a_copy(l, 1 - y).start()
        b_copy(l * depth).start()
        if l == 0:
            a_copy(l, y).start()

        @pl.loop(1, depth)
        def _(part):
            b_copy(l * depth + part).start()

        if l > 0:
            a_copy(l, y).start()

    for copy in own_copies + table_copies:
        copy.wait()

    def partial_sum(step, side):
        l, column = place(step)
        left_own = jnp.concatenate([a_own[l, side, z_of[d]] for d in range(levels)], axis=0)
        left_mate = jnp.concatenate([a_mate[l, side, z_of[d]] for d in range(levels)], axis=0)
        span = pl.ds(column, WIDTH)
        return product(left_own, b_own[l, span, :]) + product(left_mate, b_mate[l, span, :])

    def send_across(step):
        l, column = place(step)

        @pl.when(column == 0)
        def _():
            a_copy(l, 1 - y).wait()

        b_copy(step).wait()
        sums = partial_sum(step, 1 - y)
        for d in range(levels):
            coded, scale = encode(sums[d * rows : (d + 1) * rows])
            y_out[step, d] = coded
            y_out_scale[step, d : d + 1] = scale
        for copy in y_copies(step):
            copy.start()

    def send_along(step):
        l, column = place(step)

        @pl.when(column == 0)
        def _():
            a_copy(l, y).wait()

        sums = partial_sum(step, y)
        for copy in y_copies(step):
            copy.wait()
        for d in FAR_FIRST:
            block = sums[d * rows : (d + 1) * rows] + decode(
                y_in[step, d], y_in_scale[step, d : d + 1]
            )
            if d == 0:
                total[step] = block
            else:
                coded, scale = encode(block)
                z_out[step, d - 1] = coded
                z_out_scale[step, d - 1] = scale
                for copy in z_copies(step, d):
                    copy.start()

    row = lax.broadcasted_iota(jnp.int32, (rows, tile), 0) + me * rows
    lane = lax.broadcasted_iota(jnp.int32, (rows, tile), 1)

    def finish(step):
        l, first = place(step)
        live = ac_ref[l]
        block = total[step]
        for d in range(1, levels):
            for copy in z_copies(step, d):
                copy.wait()
            block = block + decode(z_in[step, d - 1], z_in_scale[step, d - 1])
        for s in range(WIDTH // tile):
            coupling = block[:, s * tile : (s + 1) * tile]
            weight = tiles[tm_ref[l, me // 2, first // tile + s]]
            column = lane + (first + s * tile)
            result = weight * coupling
            result = jnp.where(row == column, result - 2.0 * coupling, result)
            inside = (row < live) & (column < live)
            start = pl.multiple_of(l * cells + first + s * tile, tile)
            out_ref[:, pl.ds(start, tile)] = jnp.where(inside, result, 0.0)

    @pl.loop(0, steps + LAG_ALONG + LAG_FINISH)
    def _(turn):
        @pl.when(turn < steps)
        def _():
            send_across(turn)

        @pl.when((turn >= LAG_ALONG) & (turn < steps + LAG_ALONG))
        def _():
            send_along(turn - LAG_ALONG)

        @pl.when(turn >= LAG_ALONG + LAG_FINISH)
        def _():
            finish(turn - (LAG_ALONG + LAG_FINISH))


def fused_body(opacity_deriv, emission_deriv, kernel_tiles, tile_map, active_counts):
    lines, cells, bands = opacity_deriv.shape
    kinds, tile, _ = kernel_tiles.shape
    shards = lax.axis_size("band")
    rows = cells // shards
    levels = shards // 4
    steps = lines * (cells // WIDTH)
    vmem = pltpu.VMEM
    dma = pltpu.SemaphoreType.DMA
    half = jnp.bfloat16
    wide = jnp.float32
    out = pl.pallas_call(
        kernel,
        out_shape=jax.ShapeDtypeStruct((rows, lines * cells), wide),
        in_specs=[pl.BlockSpec(memory_space=pltpu.HBM)] * 5,
        out_specs=pl.BlockSpec(memory_space=pltpu.VMEM),
        scratch_shapes=[
            vmem((lines, 2, levels, rows, bands), half),
            vmem((lines, 2, levels, rows, bands), half),
            vmem((lines, cells, bands), half),
            vmem((lines, cells, bands), half),
            vmem((kinds, rows, tile), wide),
            pltpu.SMEM(tile_map.shape, tile_map.dtype),
            pltpu.SMEM(active_counts.shape, active_counts.dtype),
            vmem((steps, levels, rows, WIDTH), jnp.int16),
            vmem((steps, levels, WIDTH), wide),
            vmem((steps, levels, rows, WIDTH), jnp.int16),
            vmem((steps, levels, WIDTH), wide),
            vmem((steps, levels - 1, rows, WIDTH), jnp.int16),
            vmem((steps, levels - 1, 1, WIDTH), wide),
            vmem((steps, levels - 1, rows, WIDTH), jnp.int16),
            vmem((steps, levels - 1, 1, WIDTH), wide),
            vmem((steps, rows, WIDTH), wide),
            dma((lines, 3)),
            dma((3,)),
            dma((lines, 2)),
            dma((lines, 2)),
            dma((steps,)),
            dma((steps,)),
            dma((steps, 2)),
            dma((steps, 2)),
            dma((steps, levels - 1, 2)),
            dma((steps, levels - 1, 2)),
        ],
        compiler_params=pltpu.CompilerParams(
            collective_id=0, has_side_effects=True, vmem_limit_bytes=62 * 1024 * 1024
        ),
        cost_estimate=pl.CostEstimate(
            flops=2 * lines * cells * cells * bands,
            bytes_accessed=4 * lines * cells * bands,
            transcendentals=0,
        ),
        name="band_sum",
    )(
        opacity_deriv.reshape(lines, levels, 2, 2, rows, bands),
        emission_deriv,
        kernel_tiles,
        tile_map,
        active_counts,
    )
    return out.reshape(rows, lines, cells)


def solution(mesh):
    body = fused_body if mesh.shape["band"] == 16 else plain_body
    return jax.shard_map(
        body,
        mesh=mesh,
        in_specs=(
            P("grp", None, "band"),
            P("grp", None, "band"),
            P(),
            P("grp", None, None),
            P("grp"),
        ),
        out_specs=P("band", "grp", None),
        check_vma=False,
    )
```

time: 45.3 us -> 40.9 us (0.903)
  local copies, waits for them, and re-layouts: 6.07 us -> 2.27 us
    unnamed x10 -> x0, local copies, waits for them, and re-layouts: 4.84 us -> none
    reshape x1, local copies, waits for them, and re-layouts: 1.23 us -> 2.27 us  [fused_body(): return out.reshape(rows, lines, cells)]
where the time goes in v2:
time: 40.9 us; the launch traced here: 40.8 us
  Pallas kernels  38.5 us (94%)
  local copies, waits for them, and re-layouts  2.27 us (6%)
    pallas_call x1, Pallas kernels, fused_body(): pl.pallas_call(kernel, out_shape=jax.ShapeDtypeStruct((rows, lines * cell...  38.5 us
    reshape x1, local copies, waits for them, and re-layouts, fused_body(): return out.reshape(rows, lines, cells)  2.27 us

profile of v2, /device:TPU:0, one launch (start us, length us, event | category | flops | bytes accessed | tf_op | source)
XLA Modules:
  0.0 40.8 jit_solution(16512363210405362576)
XLA Ops:
  0.0 38.5 %band_sum.1 = f32[64,2048]{1,0:T(8,128)} custom-call(bf16[2,4,2,2,64,256]{5,4,3,2,1,0:T(8,128)(2,1)} %bitcast.1, bf16[2,1024,256]{2,1,0:T(8,128)(2,1)} %em_ref.1, f32[8,128,128]{2,1,0:T(8,128)} %kt_ref.1, s32[2,8,8]{2,1,0:T(8,128)} %map_ref.1, s32[2]{0:T(128)} %counts_ref.1), custom_call_target="tpu_custom_call" | custom-call | flops 1073741824 | bytes 2097152 | tf_op jit(solution)/shard_map/band_sum/pallas_call | solution.py:261
  38.5 2.3 %reshape.7 = f32[64,2,1024]{2,1,0:T(2,128)} reshape(f32[64,2048]{1,0:T(8,128)} %band_sum.1) | data formatting | bytes 1048576 | tf_op jit(solution)/shard_map/reshape | solution.py:310

commit v3 on v2

--- a/solution.py
+++ b/solution.py
@@ -260,7 +260,7 @@
     wide = jnp.float32
     out = pl.pallas_call(
         kernel,
-        out_shape=jax.ShapeDtypeStruct((rows, lines * cells), wide),
+        out_shape=pltpu.VMEM((rows, lines * cells), wide),
         in_specs=[pl.BlockSpec(memory_space=pltpu.HBM)] * 5,
         out_specs=pl.BlockSpec(memory_space=pltpu.VMEM),
         scratch_shapes=[

time: 40.9 us -> 39.1 us (0.956)
  local copies, waits for them, and re-layouts: 2.27 us -> 1.23 us
  Pallas kernels: 38.5 us -> 37.7 us
    reshape x1, local copies, waits for them, and re-layouts: 2.27 us -> 1.23 us  [fused_body(): return out.reshape(rows, lines, cells)]
    pallas_call x1, Pallas kernels: 38.5 us -> 37.7 us  [fused_body(): pl.pallas_call(kernel, out_shape=pltpu.VMEM((rows, lines * cells), wide),...]
where the time goes in v3:
time: 39.1 us; the launch traced here: 38.9 us
  Pallas kernels  37.7 us (96%)
  local copies, waits for them, and re-layouts  1.23 us (3%)
    pallas_call x1, Pallas kernels, fused_body(): pl.pallas_call(kernel, out_shape=pltpu.VMEM((rows, lines * cells), wide),...  37.7 us
    reshape x1, local copies, waits for them, and re-layouts, fused_body(): return out.reshape(rows, lines, cells)  1.23 us

profile of v3, /device:TPU:0, one launch (start us, length us, event | category | flops | bytes accessed | tf_op | source)
XLA Modules:
  0.0 38.9 jit_solution(4256586804470532791)
XLA Ops:
  0.0 37.7 %band_sum.1 = f32[64,2048]{1,0:T(8,128)S(1)} custom-call(bf16[2,4,2,2,64,256]{5,4,3,2,1,0:T(8,128)(2,1)} %bitcast.1, bf16[2,1024,256]{2,1,0:T(8,128)(2,1)} %em_ref.1, f32[8,128,128]{2,1,0:T(8,128)} %kt_ref.1, s32[2,8,8]{2,1,0:T(8,128)} %map_ref.1, s32[2]{0:T(128)} %counts_ref.1), custom_call_target="tpu_custom_call" | custom-call | flops 1073741824 | bytes 2097152 | tf_op jit(solution)/shard_map/band_sum/pallas_call | solution.py:261
  37.7 1.2 %reshape.7 = f32[64,2,1024]{2,1,0:T(2,128)} reshape(f32[64,2048]{1,0:T(8,128)S(1)} %band_sum.1) | data formatting | bytes 1048576 | tf_op jit(solution)/shard_map/reshape | solution.py:310

commit v4 on v3

--- a/solution.py
+++ b/solution.py
@@ -13,6 +13,7 @@
 WIDTH = 256
 LAG_ALONG = 2
 LAG_FINISH = 2
+FIRST_ACROSS = 5
 FAR_FIRST = (2, 1, 3, 0)
 
 
@@ -67,7 +68,9 @@
     a_own, a_mate, b_own, b_mate, tiles, tm_ref, ac_ref,
     y_out, y_out_scale, y_in, y_in_scale,
     z_out, z_out_scale, z_in, z_in_scale, total,
+    f_out, f_out_scale, f_in, f_in_scale, f_own, c_out, c_out_scale, c_in, c_in_scale,
     own_sem, table_sem, a_send, a_recv, b_send, b_recv, y_send, y_recv, z_send, z_recv,
+    f_send, f_recv, c_send, c_recv,
 ):
     lines, cells = em_ref.shape[0], em_ref.shape[1]
     levels, rows = op_ref.shape[1], op_ref.shape[4]
@@ -149,13 +152,38 @@
             ),
         )
 
+    def f_copies(d):
+        return (
+            pltpu.make_async_remote_copy(
+                f_out.at[d - 1], f_in.at[d - 1], f_send.at[d - 1, 0], f_recv.at[d - 1, 0],
+                device_id={"band": along[d]}, device_id_type=MESH,
+            ),
+            pltpu.make_async_remote_copy(
+                f_out_scale.at[d - 1], f_in_scale.at[d - 1],
+                f_send.at[d - 1, 1], f_recv.at[d - 1, 1],
+                device_id={"band": along[d]}, device_id_type=MESH,
+            ),
+        )
+
+    c_copies = (
+        pltpu.make_async_remote_copy(
+            c_out, c_in, c_send.at[0], c_recv.at[0],
+            device_id={"band": across}, device_id_type=MESH,
+        ),
+        pltpu.make_async_remote_copy(
+            c_out_scale, c_in_scale, c_send.at[1], c_recv.at[1],
+            device_id={"band": across}, device_id_type=MESH,
+        ),
+    )
+
     for l in range(lines):
         a_copy(l, 1 - y).start()
         b_copy(l * depth).start()
         if l == 0:
+            b_copy(1).start()
             a_copy(l, y).start()
 
-        @pl.loop(1, depth)
+        @pl.loop(2 if l == 0 else 1, depth)
         def _(part):
             b_copy(l * depth + part).start()
 
@@ -175,7 +203,7 @@
     def send_across(step):
         l, column = place(step)
 
-        @pl.when(column == 0)
+        @pl.when((column == 0) & (l > 0))
         def _():
             a_copy(l, 1 - y).wait()
 
@@ -191,7 +219,7 @@
     def send_along(step):
         l, column = place(step)
 
-        @pl.when(column == 0)
+        @pl.when((column == 0) & (l > 0))
         def _():
             a_copy(l, y).wait()
 
@@ -214,14 +242,9 @@
     row = lax.broadcasted_iota(jnp.int32, (rows, tile), 0) + me * rows
     lane = lax.broadcasted_iota(jnp.int32, (rows, tile), 1)
 
-    def finish(step):
+    def emit(step, block):
         l, first = place(step)
         live = ac_ref[l]
-        block = total[step]
-        for d in range(1, levels):
-            for copy in z_copies(step, d):
-                copy.wait()
-            block = block + decode(z_in[step, d - 1], z_in_scale[step, d - 1])
         for s in range(WIDTH // tile):
             coupling = block[:, s * tile : (s + 1) * tile]
             weight = tiles[tm_ref[l, me // 2, first // tile + s]]
@@ -232,19 +255,72 @@
             start = pl.multiple_of(l * cells + first + s * tile, tile)
             out_ref[:, pl.ds(start, tile)] = jnp.where(inside, result, 0.0)
 
-    @pl.loop(0, steps + LAG_ALONG + LAG_FINISH)
+    def finish(step):
+        block = total[step]
+        for d in range(1, levels):
+            for copy in z_copies(step, d):
+                copy.wait()
+            block = block + decode(z_in[step, d - 1], z_in_scale[step, d - 1])
+        emit(step, block)
+
+    def first_along():
+        a_copy(0, y).wait()
+        b_copy(0).wait()
+        for side in range(2):
+            sums = partial_sum(0, side)
+            f_own[side] = sums[:rows]
+            for d in range(1, levels):
+                coded, scale = encode(sums[d * rows : (d + 1) * rows])
+                f_out[d - 1, side] = coded
+                f_out_scale[d - 1, side] = scale
+        for d in FAR_FIRST[:-1]:
+            for copy in f_copies(d):
+                copy.start()
+
+    def first_sum(side):
+        block = f_own[side]
+        for d in range(1, levels):
+            block = block + decode(f_in[d - 1, side], f_in_scale[d - 1, side])
+        return block
+
+    def first_across():
+        for d in range(1, levels):
+            for copy in f_copies(d):
+                copy.wait()
+        coded, scale = encode(first_sum(1 - y))
+        c_out[...] = coded
+        c_out_scale[...] = scale
+        for copy in c_copies:
+            copy.start()
+
+    a_copy(0, 1 - y).wait()
+    send_across(1)
+    first_along()
+    send_across(2)
+
+    @pl.loop(3, steps + LAG_ALONG + LAG_FINISH)
     def _(turn):
         @pl.when(turn < steps)
         def _():
             send_across(turn)
 
-        @pl.when((turn >= LAG_ALONG) & (turn < steps + LAG_ALONG))
+        @pl.when((turn > LAG_ALONG) & (turn < steps + LAG_ALONG))
         def _():
             send_along(turn - LAG_ALONG)
 
-        @pl.when(turn >= LAG_ALONG + LAG_FINISH)
+        @pl.when(turn == FIRST_ACROSS)
+        def _():
+            first_across()
+
+        @pl.when(turn > LAG_ALONG + LAG_FINISH)
         def _():
             finish(turn - (LAG_ALONG + LAG_FINISH))
+
+        @pl.when(turn == steps)
+        def _():
+            for copy in c_copies:
+                copy.wait()
+            emit(0, first_sum(y) + decode(c_in[...], c_in_scale[...]))
 
 
 def fused_body(opacity_deriv, emission_deriv, kernel_tiles, tile_map, active_counts):
@@ -280,6 +356,15 @@
             vmem((steps, levels - 1, rows, WIDTH), jnp.int16),
             vmem((steps, levels - 1, 1, WIDTH), wide),
             vmem((steps, rows, WIDTH), wide),
+            vmem((levels - 1, 2, rows, WIDTH), jnp.int16),
+            vmem((levels - 1, 2, 1, WIDTH), wide),
+            vmem((levels - 1, 2, rows, WIDTH), jnp.int16),
+            vmem((levels - 1, 2, 1, WIDTH), wide),
+            vmem((2, rows, WIDTH), wide),
+            vmem((rows, WIDTH), jnp.int16),
+            vmem((1, WIDTH), wide),
+            vmem((rows, WIDTH), jnp.int16),
+            vmem((1, WIDTH), wide),
             dma((lines, 3)),
             dma((3,)),
             dma((lines, 2)),
@@ -290,6 +375,10 @@
             dma((steps, 2)),
             dma((steps, levels - 1, 2)),
             dma((steps, levels - 1, 2)),
+            dma((levels - 1, 2)),
+            dma((levels - 1, 2)),
+            dma((2,)),
+            dma((2,)),
         ],
         compiler_params=pltpu.CompilerParams(
             collective_id=0, has_side_effects=True, vmem_limit_bytes=62 * 1024 * 1024

time: 39.1 us -> 37.8 us (0.967)
  Pallas kernels: 37.7 us -> 36.5 us
    pallas_call x1, Pallas kernels: 37.7 us -> 36.5 us  [fused_body(): pl.pallas_call(kernel, out_shape=pltpu.VMEM((rows, lines * cells), wide),...]
where the time goes in v4:
time: 37.8 us; the launch traced here: 37.7 us
  Pallas kernels  36.5 us (97%)
  local copies, waits for them, and re-layouts  1.23 us (3%)
    pallas_call x1, Pallas kernels, fused_body(): pl.pallas_call(kernel, out_shape=pltpu.VMEM((rows, lines * cells), wide),...  36.5 us
    reshape x1, local copies, waits for them, and re-layouts, fused_body(): return out.reshape(rows, lines, cells)  1.23 us

profile of v4, /device:TPU:0, one launch (start us, length us, event | category | flops | bytes accessed | tf_op | source)
XLA Modules:
  0.0 37.7 jit_solution(16114225890227015850)
XLA Ops:
  0.0 36.5 %band_sum.1 = f32[64,2048]{1,0:T(8,128)S(1)} custom-call(bf16[2,4,2,2,64,256]{5,4,3,2,1,0:T(8,128)(2,1)} %bitcast.1, bf16[2,1024,256]{2,1,0:T(8,128)(2,1)} %em_ref.1, f32[8,128,128]{2,1,0:T(8,128)} %kt_ref.1, s32[2,8,8]{2,1,0:T(8,128)} %map_ref.1, s32[2]{0:T(128)} %counts_ref.1), custom_call_target="tpu_custom_call" | custom-call | flops 1073741824 | bytes 2097152 | tf_op jit(solution)/shard_map/band_sum/pallas_call | solution.py:337
  36.5 1.2 %reshape.7 = f32[64,2,1024]{2,1,0:T(2,128)} reshape(f32[64,2048]{1,0:T(8,128)S(1)} %band_sum.1) | data formatting | bytes 1048576 | tf_op jit(solution)/shard_map/reshape | solution.py:399

commit v5 on v4

--- a/solution.py
+++ b/solution.py
@@ -294,8 +294,8 @@
             copy.start()
 
     a_copy(0, 1 - y).wait()
+    first_along()
     send_across(1)
-    first_along()
     send_across(2)
 
     @pl.loop(3, steps + LAG_ALONG + LAG_FINISH)

time: 37.8 us -> 37.9 us (level)
  no operation moved by 1% of the time
where the time goes in v5:
time: 37.9 us; the launch traced here: 37.8 us
  Pallas kernels  36.5 us (96%)
  local copies, waits for them, and re-layouts  1.23 us (3%)
    pallas_call x1, Pallas kernels, fused_body(): pl.pallas_call(kernel, out_shape=pltpu.VMEM((rows, lines * cells), wide),...  36.5 us
    reshape x1, local copies, waits for them, and re-layouts, fused_body(): return out.reshape(rows, lines, cells)  1.23 us

profile of v5, /device:TPU:0, one launch (start us, length us, event | category | flops | bytes accessed | tf_op | source)
XLA Modules:
  0.0 37.8 jit_solution(12572469631654654880)
XLA Ops:
  0.0 36.5 %band_sum.1 = f32[64,2048]{1,0:T(8,128)S(1)} custom-call(bf16[2,4,2,2,64,256]{5,4,3,2,1,0:T(8,128)(2,1)} %bitcast.1, bf16[2,1024,256]{2,1,0:T(8,128)(2,1)} %em_ref.1, f32[8,128,128]{2,1,0:T(8,128)} %kt_ref.1, s32[2,8,8]{2,1,0:T(8,128)} %map_ref.1, s32[2]{0:T(128)} %counts_ref.1), custom_call_target="tpu_custom_call" | custom-call | flops 1073741824 | bytes 2097152 | tf_op jit(solution)/shard_map/band_sum/pallas_call | solution.py:337
  36.5 1.2 %reshape.7 = f32[64,2,1024]{2,1,0:T(2,128)} reshape(f32[64,2048]{1,0:T(8,128)S(1)} %band_sum.1) | data formatting | bytes 1048576 | tf_op jit(solution)/shard_map/reshape | solution.py:399
